TPU v7x, 128 devices: a whole 4x4x4 slice. The times are simulated.
128 devices in a mesh: ctx: 16 (over y_hi, x, core), head: 8 (over z, y_lo).
Axes of the slice: x: 4, y: 4 (y_hi: 2, y_lo: 2; y = y_hi * 2 + y_lo), z: 4, core: 2. Of those that a mesh axis runs over, the one named last changes fastest.
Arguments:
- queries: bfloat16 [16384, 4096], P('ctx', 'head'), may hold values from -170 to 170
- keys_full: bfloat16 [16384, 4096], P('ctx', 'head'), may hold values from -6 to 6
- values_full: bfloat16 [16384, 4096], P('ctx', 'head'), may hold values from -6 to 6
- keys_proj: bfloat16 [1024, 4096], P(None, 'head'), may hold values from -7 to 7
- values_proj: bfloat16 [1024, 4096], P(None, 'head'), may hold values from -6 to 6
- key_factor: bfloat16 [16384, 1024], P('ctx'), may hold values from -0.1875 to 0.1875
- value_factor: bfloat16 [16384, 1024], P('ctx'), may hold values from -0.1875 to 0.1875
- out_grad: bfloat16 [16384, 4096], P('ctx', 'head'), may hold values from -6 to 6
Outputs:
- grad_queries: bfloat16 [16384, 4096], P('ctx', 'head')
- grad_keys: bfloat16 [16384, 4096], P('ctx', 'head')
- grad_values: bfloat16 [16384, 4096], P('ctx', 'head')
- grad_kfactor: bfloat16 [16384, 1024], P('ctx', 'head')
- grad_vfactor: bfloat16 [16384, 1024], P('ctx', 'head')
All inputs are finite; a program needn't handle non-finite values.
Results may differ from a plain program's by a relative error of at most 0.008.
Values may be sent and summed in bfloat16 or wider, within the bound.
A program may use at most 128 MiB of HBM per device.

v0:
```python
import jax
import jax.numpy as jnp
from jax import lax
from jax.sharding import PartitionSpec as P

DH = 128


def per_device(
    queries, keys_full, values_full, keys_proj, values_proj, key_factor, value_factor, out_grad
):
    scale = DH ** (-0.5)
    tok_rows = queries.shape[0]
    heads_here = queries.shape[1] // DH
    proj_rows = keys_proj.shape[0]
    query_blocks = queries.reshape(tok_rows, heads_here, DH)
    grad_blocks = out_grad.reshape(tok_rows, heads_here, DH)
    key_blocks = keys_proj.reshape(proj_rows, heads_here, DH)
    value_blocks = values_proj.reshape(proj_rows, heads_here, DH)
    scores = (
        jnp.einsum("nhd,rhd->hnr", query_blocks, key_blocks, preferred_element_type=jnp.float32)
        * scale
    )
    probs = jax.nn.softmax(scores, axis=-1)
    probs_low = probs.astype(jnp.bfloat16)
    attn_out = jnp.einsum(
        "hnr,rhd->nhd", probs_low, value_blocks, preferred_element_type=jnp.float32
    )
    dprobs = jnp.einsum(
        "nhd,rhd->hnr", grad_blocks, value_blocks, preferred_element_type=jnp.float32
    )
    delta = jnp.sum(grad_blocks.astype(jnp.float32) * attn_out, axis=-1)
    delta = jnp.transpose(delta, (1, 0))[:, :, None]
    dscores = (probs * (dprobs - delta) * scale).astype(jnp.bfloat16)
    dkp_part = jnp.einsum(
        "hnr,nhd->rhd", dscores, query_blocks, preferred_element_type=jnp.float32
    ).reshape(proj_rows, heads_here * DH)
    dvp_part = jnp.einsum(
        "hnr,nhd->rhd", probs_low, grad_blocks, preferred_element_type=jnp.float32
    ).reshape(proj_rows, heads_here * DH)
    grad_queries = jnp.einsum(
        "hnr,rhd->nhd", dscores, key_blocks, preferred_element_type=jnp.float32
    )
    grad_queries = grad_queries.astype(jnp.bfloat16).reshape(tok_rows, heads_here * DH)
    dkp_sum, dvp_sum = lax.psum((dkp_part, dvp_part), "ctx")
    dkp_low = dkp_sum.astype(jnp.bfloat16)
    dvp_low = dvp_sum.astype(jnp.bfloat16)
    grad_keys = jnp.dot(key_factor, dkp_low, preferred_element_type=jnp.float32).astype(
        jnp.bfloat16
    )
    grad_values = jnp.dot(value_factor, dvp_low, preferred_element_type=jnp.float32).astype(
        jnp.bfloat16
    )
    kfactor_part = jnp.einsum("nc,rc->nr", keys_full, dkp_low, preferred_element_type=jnp.float32)
    vfactor_part = jnp.einsum("nc,rc->nr", values_full, dvp_low, preferred_element_type=jnp.float32)
    kfactor_sum, vfactor_sum = (
        lax.psum_scatter(kfactor_part, "head", scatter_dimension=1, tiled=True),
        lax.psum_scatter(vfactor_part, "head", scatter_dimension=1, tiled=True),
    )
    return (
        grad_queries,
        grad_keys,
        grad_values,
        kfactor_sum.astype(jnp.bfloat16),
        vfactor_sum.astype(jnp.bfloat16),
    )


def solution(mesh):
    placed = (
        P("ctx", "head"),
        P("ctx", "head"),
        P("ctx", "head"),
        P(None, "head"),
        P(None, "head"),
        P("ctx", None),
        P("ctx", None),
        P("ctx", "head"),
    )
    return jax.shard_map(
        per_device,
        mesh=mesh,
        in_specs=placed,
        out_specs=(
            P("ctx", "head"),
            P("ctx", "head"),
            P("ctx", "head"),
            P("ctx", "head"),
            P("ctx", "head"),
        ),
        check_vma=False,
    )
```

profile of v0, /device:TPU:1, one launch (start us, length us, event | category | flops | bytes accessed | tf_op | source)
XLA Modules:
  0.0 337.7 jit_solution(649763854368210690)
XLA Ops:
  7.2 0.0 copy-start
  7.2 0.0 reduce-scatter.5.cloned.1.call-start
  7.2 2.4 copy.38
  9.6 2.3 copy.37
  11.9 2.3 copy.39
  14.2 1.5 copy.15
  15.7 10.1 %fusion.16 = (f32[4,1024]{1,0:T(4,128)S(1)}, f32[4,1024,1024]{1,2,0:T(8,128)}) fusion(bf16[1024,4,128]{0,2,1:T(8,128)(2,1)} %bitcast.58, bf16[1024,4,128]{0,2,1:T(8,128)(2,1)} %bitcast.53), kind=kOutput, calls=%fused_computation.23 | convolution fusion | flops 1086325760 | bytes 18890752 | tf_op jit(solution)/shard_map/sub | solution.py:24
  25.7 6.9 %fusion.5 = bf16[4,1024,1024]{1,2,0:T(8,128)(2,1)S(1)} fusion(f32[4,1024,1024]{1,2,0:T(8,128)} %get-tuple-element.13, f32[4,1024]{1,0:T(4,128)S(1)} %get-tuple-element.12), kind=kLoop, calls=%fused_computation.7 | loop fusion | flops 8388608 | bytes 25182208 | tf_op jit(solution)/shard_map/convert_element_type | solution.py:25
  32.7 0.0 copy-start.3
  32.7 4.3 %fusion.18 = f32[4,1024,128]{1,2,0:T(8,128)} fusion(bf16[4,1024,1024]{1,2,0:T(8,128)(2,1)S(1)} %fusion.5, bf16[1024,4,128]{0,2,1:T(8,128)(2,1)S(1)} %bitcast.48), kind=kOutput, calls=%fused_computation.25 | convolution fusion | flops 1073741824 | bytes 11534336 | tf_op jit(solution)/shard_map/hnr,nhd->rhd/dot_general | solution.py:38
  36.9 1.4 fusion.6
  38.4 7.4 %multiply_convert_fusion = bf16[4,1024,1024]{1,2,0:T(8,128)(2,1)S(1)} fusion(bf16[1024,4,128]{0,2,1:T(8,128)(2,1)S(1)} %bitcast.56, bf16[1024,4,128]{0,2,1:T(8,128)(2,1)S(1)} %bitcast.50, f32[4,1024]{1,0:T(4,128)S(1)} %bitcast.60, f32[4,1024,1024]{1,2,0:T(8,128)} %get-tuple-element.13, f32[4,1024]{1,0:T(4,128)S(1)} %get-tuple-element.12), kind=kOutput, calls=%fused_computation.1 | convolution fusion | flops 1094713344 | bytes 27295744 | tf_op jit(solution)/shard_map/nhd,rhd->hnr/dot_general | solution.py:29
  45.9 3.2 copy-done.1
  49.1 4.3 %fusion.17 = f32[4,1024,128]{1,2,0:T(8,128)} fusion(bf16[4,1024,1024]{1,2,0:T(8,128)(2,1)S(1)} %multiply_convert_fusion, bf16[1024,4,128]{0,2,1:T(8,128)(2,1)S(1)} %bitcast.59), kind=kOutput, calls=%fused_computation.24 | convolution fusion | flops 1073741824 | bytes 11534336 | tf_op jit(solution)/shard_map/hnr,nhd->rhd/dot_general | solution.py:35
  53.4 83.5 %all-reduce.2 = (bf16[1024,512]{0,1:T(8,128)(2,1)}, bf16[1024,512]{0,1:T(8,128)(2,1)}) all-reduce(f32[1024,512]{0,1:T(8,128)} %bitcast.52, f32[1024,512]{0,1:T(8,128)} %bitcast.51), channel_id=1, replica_groups=mesh['ctx'=16,'head'=8] {'ctx'}, use_global_device_ids=true, to_apply=%region_3.0 | all-reduce | flops 1048576 | bytes 6291456 | tf_op jit(solution)/shard_map/psum | solution.py:45
  136.8 4.5 %convolution_bitcast_fusion = f32[1024,1024]{0,1:T(8,128)} fusion(bf16[1024,512]{1,0:T(8,128)(2,1)S(1)} %copy-done.5, bf16[1024,512]{0,1:T(8,128)(2,1)} %get-tuple-element.11), kind=kOutput, calls=%fused_computation.8 | convolution fusion | flops 1073741824 | bytes 6291456 | tf_op jit(solution)/shard_map/nc,rc->nr/dot_general | solution.py:55
  141.3 0.0 reduce-scatter.5.cloned.1.call-update
  141.4 0.0 reduce-scatter.3.cloned.1.call-start
  141.4 4.9 %convolution_bitcast_fusion.1 = f32[1024,1024]{0,1:T(8,128)} fusion(bf16[1024,512]{1,0:T(8,128)(2,1)} %param.9, bf16[1024,512]{0,1:T(8,128)(2,1)} %get-tuple-element.10), kind=kOutput, calls=%fused_computation.9 | convolution fusion | flops 1073741824 | bytes 6291456 | tf_op jit(solution)/shard_map/nc,rc->nr/dot_general | solution.py:54
  146.3 0.0 reduce-scatter.3.cloned.1.call-update
  146.3 5.6 %convolution_convert_fusion.2 = bf16[4,1024,128]{1,2,0:T(8,128)(2,1)} fusion(bf16[1024,4,128]{0,2,1:T(8,128)(2,1)S(1)} %bitcast.54, bf16[4,1024,1024]{1,2,0:T(8,128)(2,1)} %copy-done.1), kind=kOutput, calls=%fused_computation.14 | convolution fusion | flops 1074266112 | bytes 10485760 | tf_op jit(solution)/shard_map/hnr,rhd->nhd/dot_general | solution.py:41
  152.0 2.4 copy.26
  154.3 2.5 fusion.7
  156.8 1.3 copy.27
  158.2 3.2 fusion.8
  161.4 1.3 copy.28
  162.7 72.5 %reduce-scatter.5.cloned.1.call-done = f32[1024,128]{0,1:T(8,128)} async-done(((f32[1024,1024]{0,1:T(8,128)}), f32[1024,128]{0,1:T(8,128)}) %reduce-scatter.5.cloned.1.call-update) | async-done | bytes 524304 | tf_op jit(solution)/shard_map/reduce_scatter | solution.py:58
  235.3 1.1 convert_element_type.51
  236.3 0.8 copy.30
  237.2 91.8 %reduce-scatter.3.cloned.1.call-done = f32[1024,128]{0,1:T(8,128)} async-done(((f32[1024,1024]{0,1:T(8,128)}), f32[1024,128]{0,1:T(8,128)}) %reduce-scatter.3.cloned.1.call-update) | async-done | bytes 524304 | tf_op jit(solution)/shard_map/reduce_scatter | solution.py:57
  329.0 1.1 convert_element_type.50
  330.1 0.8 copy.29
  (9 shorter events, 0.0 us)
Async XLA Ops:
  7.2 147.2 %copy-start = (bf16[1024,1024]{1,0:T(8,128)(2,1)S(1)}, bf16[1024,1024]{1,0:T(8,128)(2,1)}, u32[]{:S(2)}) copy-start(bf16[1024,1024]{1,0:T(8,128)(2,1)} %param.13) | copy-start | bytes 6291460
  7.2 228.1 %reduce-scatter.5.cloned.1.call-start = ((), (), s32[]{:S(2)}) async-start(), calls=%async_computation.3 | async-start | bytes 4718592 | tf_op jit(solution)/shard_map/reduce_scatter | solution.py:58
  32.7 4.3 %copy-start.3 = (bf16[1024,512]{0,1:T(8,128)(2,1)S(1)}, bf16[1024,512]{0,1:T(8,128)(2,1)}, u32[]{:S(2)}) copy-start(bf16[1024,512]{0,1:T(8,128)(2,1)} %copy.39) | copy-start | bytes 3145732
  38.4 10.7 %copy-start.4 = (bf16[1024,512]{0,1:T(8,128)(2,1)S(1)}, bf16[1024,512]{0,1:T(8,128)(2,1)}, u32[]{:S(2)}) copy-start(bf16[1024,512]{0,1:T(8,128)(2,1)} %copy.38) | copy-start | bytes 3145732
  45.8 3.2 copy-start.1
  49.1 87.8 %copy-start.5 = (bf16[1024,512]{1,0:T(8,128)(2,1)S(1)}, bf16[1024,512]{1,0:T(8,128)(2,1)}, u32[]{:S(2)}) copy-start(bf16[1024,512]{1,0:T(8,128)(2,1)} %param.10) | copy-start | bytes 3145732
  141.3 5.0 %copy-start.2 = (bf16[1024,512]{0,1:T(8,128)(2,1)S(1)}, bf16[1024,512]{0,1:T(8,128)(2,1)}, u32[]{:S(2)}) copy-start(bf16[1024,512]{0,1:T(8,128)(2,1)} %copy.37) | copy-start | bytes 3145732
  141.4 187.6 %reduce-scatter.3.cloned.1.call-start = ((), (), s32[]{:S(2)}) async-start(), calls=%async_computation.2 | async-start | bytes 4718592 | tf_op jit(solution)/shard_map/reduce_scatter | solution.py:57
Sparse Core Ops, SparseCore 0:
  141.5 93.7 reduce-scatter.4
  237.7 91.2 reduce-scatter.2
where the time goes:
time: 338 us
  waiting for transfers between devices  164 us (49%)
  blocking collectives  83.5 us (25%)
  matrix products  48.3 us (14%)
  local copies, waits for them, and re-layouts  18.4 us (5%)
  between operations  14.1 us (4%)
  other arithmetic  9.07 us (3%)
    reduce_scatter x1, waiting for transfers between devices, per_device(): lax.psum_scatter(kfactor_part, 'head', scatter_dimension=1, tiled=True)  91.8 us
    psum x1, blocking collectives, per_device(): dkp_sum, dvp_sum = lax.psum((dkp_part, dvp_part), 'ctx')  83.5 us
    reduce_scatter x1, waiting for transfers between devices, per_device(): lax.psum_scatter(vfactor_part, 'head', scatter_dimension=1, tiled=True)  72.5 us
    unnamed x18, local copies, waits for them, and re-layouts  11.4 us
    sub x1, matrix products, per_device(): probs = jax.nn.softmax(scores, axis=-1)  10.1 us
    dot_general x1, matrix products, per_device(): jnp.einsum('nhd,rhd->hnr', grad_blocks, value_blocks, preferred_element_t...  7.45 us
    convert_element_type x1, other arithmetic, per_device(): probs_low = probs.astype(jnp.bfloat16)  6.93 us
  transfers between devices with their start and end apart: 2, of which 2 were waited for; matrix products, arithmetic and copies ran while one was open for 7% of the time, Pallas kernels for 0%

commit v1 on v0

v1 whole, which is shorter than its diff:
```python
import functools

import jax
import jax.numpy as jnp
from jax import lax
from jax.experimental import pallas as pl
from jax.experimental.pallas import tpu as pltpu
from jax.sharding import PartitionSpec as P

DH = 128
SCALE = DH ** (-0.5)
SCALE_LOG2 = SCALE * 1.4426950408889634
BF = jnp.bfloat16
F32 = jnp.float32
MESH = pl.DeviceIdType.MESH
NT = (((1,), (1,)), ((), ()))

TOK = 1024
ROWS = 1024
COLS = 512
HALF = ROWS // 2
BLK = HALF // 8
R1 = 512
R2 = TOK - R1

CORE, RS, AG, FWD, Z1, Y1, Y2, Z2, NSEM = 0, 1, 8, 15, 16, 19, 20, 21, 24


def kernel(
    q_h, kf_h, vf_h, kp_h, vp_h, e_h, f_h, do_h,
    gq_h, gk_h, gv_h, gkf_h, gvf_h,
    q, kf, vf, kp, vp, ef, ff, do,
    probs, acc, xs, xr, rs, rr, ag, partz, party, zr, yr, own1, ys2, yr2, zs2, zr2,
    gq, gk, gv, gfac, in_sem, out_sem, ssem, rsem,
):
    ctx = lax.axis_index("ctx")
    head = lax.axis_index("head")
    yh, x, core = ctx // 8, (ctx // 2) % 4, ctx % 2
    z, yl = head // 2, head % 2
    chip = yh * 4 + x

    def ctx_dev(i):
        dy, dx = (i + 1) // 4, (i + 1) % 4
        py, px = (yh + dy) % 2, (x + dx) % 4
        return py * 4 + px, (py * 8 + px * 2 + core, head)

    def z_dev(d):
        pz = (z + d) % 4
        return pz, (ctx, pz * 2 + yl)

    other_core = (yh * 8 + x * 2 + (1 - core), head)
    other_yl = (ctx, z * 2 + (1 - yl))

    bar = pltpu.get_barrier_semaphore()
    peers = [other_core, other_yl] + [ctx_dev(i)[1] for i in range(7)]
    peers += [z_dev(d)[1] for d in (1, 2, 3)]
    for p in peers:
        pl.semaphore_signal(bar, inc=1, device_id=p, device_id_type=MESH)

    loads = {}
    for i, (name, src, dst) in enumerate((
        ("q", q_h, q), ("kp", kp_h, kp), ("do", do_h, do), ("vp", vp_h, vp),
        ("vf", vf_h, vf), ("ff", f_h, ff), ("kf", kf_h, kf), ("ef", e_h, ef),
    )):
        loads[name] = pltpu.make_async_copy(src, dst, in_sem.at[i])
        loads[name].start()

    def cols(h):
        return slice(h * DH, (h + 1) * DH)

    def stage_a(h):
        s = lax.dot_general(kp[:, cols(h)], q[:, cols(h)], NT, preferred_element_type=F32)
        m = jnp.max(s, axis=0, keepdims=True)
        e = jnp.exp2((s - m) * SCALE_LOG2)
        l = jnp.sum(e, axis=0, keepdims=True)
        p = e * (1.0 / l)
        probs[h] = p
        acc[0, :, cols(h)] = jnp.dot(p.astype(BF), do[:, cols(h)], preferred_element_type=F32)

    def stage_b(h):
        dp = lax.dot_general(vp[:, cols(h)], do[:, cols(h)], NT, preferred_element_type=F32)
        p = probs[h]
        delta = jnp.sum(p.astype(BF).astype(F32) * dp, axis=0, keepdims=True)
        ds = (p * (dp - delta) * SCALE).astype(BF)
        acc[1, :, cols(h)] = jnp.dot(ds, q[:, cols(h)], preferred_element_type=F32)
        g = jnp.dot(kp[:, cols(h)].T, ds, preferred_element_type=F32)
        gq[:, cols(h)] = g.T.astype(BF)

    sent = []

    def remote(src, dst, w, slot, dev):
        cp = pltpu.make_async_remote_copy(
            src, dst, ssem.at[w, slot], rsem.at[w, slot], device_id=dev, device_id_type=MESH
        )
        cp.start()
        sent.append(cp)
        return cp

    mine = pl.multiple_of(core * HALF, HALF)
    theirs = pl.multiple_of((1 - core) * HALF, HALF)
    own_row = pl.multiple_of(core * HALF + chip * BLK, BLK)
    own_blk = pl.multiple_of(chip * BLK, BLK)

    def swap_cores(w):
        xs[w] = acc[w, pl.ds(theirs, HALF), :].astype(BF)
        return [remote(xs.at[w], xr.at[w], w, CORE, other_core)]

    def scatter(w, before):
        before[0].wait_recv()
        rs[w] = (acc[w, pl.ds(mine, HALF), :] + xr[w].astype(F32)).astype(BF)
        out = []
        for i in range(7):
            pc, dev = ctx_dev(i)
            src = rs.at[w, pl.ds(pl.multiple_of(pc * BLK, BLK), BLK), :]
            out.append(remote(src, rr.at[w, i], w, RS + i, dev))
        return out

    def gather(w, before):
        for cp in before:
            cp.wait_recv()
        total = rs[w, pl.ds(own_blk, BLK), :].astype(F32)
        for i in range(7):
            total = total + rr[w, i].astype(F32)
        ag[w, pl.ds(own_row, BLK), :] = total.astype(BF)
        block = ag.at[w, pl.ds(own_row, BLK), :]
        return [remote(block, block, w, AG + i, ctx_dev(i)[1]) for i in range(7)]

    def forward(w, before):
        for cp in before:
            cp.wait_recv()
        block = ag.at[w, pl.ds(mine, HALF), :]
        return [remote(block, block, w, FWD, other_core)]

    def factor(w, full, before):
        before[0].wait_recv()
        part = lax.dot_general(full[R1:, :], ag[w], NT, preferred_element_type=F32)
        for pz in range(4):
            for py in range(2):
                j = pz * 2 + py
                party[w, py * 4 + pz] = part[:, j * DH : (j + 1) * DH].astype(BF)
        y1 = remote(party.at[w, pl.ds((1 - yl) * 4, 4)], yr.at[w], w, Y1, other_yl)
        part = lax.dot_general(full[:R1, :], ag[w], NT, preferred_element_type=F32)
        for j in range(8):
            partz[w, j] = part[:, j * DH : (j + 1) * DH].astype(BF)
        z1 = []
        for d in (1, 2, 3):
            pz, dev = z_dev(d)
            z1.append(remote(partz.at[w, pl.ds(pz * 2, 2)], zr.at[w, d - 1], w, Z1 + d - 1, dev))
        return [y1], z1

    def second_z(w, before):
        for cp in before:
            cp.wait_recv()
        for k in range(4):
            zs2[w, k] = (party[w, yl * 4 + k].astype(F32) + yr[w, k].astype(F32)).astype(BF)
        out = []
        for d in (1, 2, 3):
            pz, dev = z_dev(d)
            out.append(remote(zs2.at[w, pz], zr2.at[w, d - 1], w, Z2 + d - 1, dev))
        return out

    def second_y(w, before):
        for cp in before:
            cp.wait_recv()

        def total(b):
            t = partz[w, z * 2 + b].astype(F32)
            for d in range(3):
                t = t + zr[w, d, b].astype(F32)
            return t

        ys2[w] = total(1 - yl).astype(BF)
        out = [remote(ys2.at[w], yr2.at[w], w, Y2, other_yl)]
        own1[w] = total(yl)
        return out

    def finish(w, y2, z2):
        for cp in y2:
            cp.wait_recv()
        gfac[w, :R1, :] = (own1[w] + yr2[w].astype(F32)).astype(BF)
        for cp in z2:
            cp.wait_recv()
        t = zs2[w, z].astype(F32)
        for d in range(3):
            t = t + zr2[w, d].astype(F32)
        gfac[w, R1:, :] = t.astype(BF)

    outs = []

    def store(src, dst):
        cp = pltpu.make_async_copy(src, dst, out_sem.at[len(outs)])
        cp.start()
        outs.append(cp)

    for name in ("q", "kp", "do"):
        loads[name].wait()
    for h in range(4):
        stage_a(h)
    pl.semaphore_wait(bar, len(peers))
    v = swap_cores(0)
    loads["vp"].wait()
    stage_b(0)
    v = scatter(0, v)
    stage_b(1)
    v = gather(0, v)
    stage_b(2)
    v = forward(0, v)
    stage_b(3)
    k = swap_cores(1)
    store(gq, gq_h)
    loads["vf"].wait()
    vy1, vz1 = factor(0, vf, v)
    k = scatter(1, k)
    loads["ff"].wait()
    gv[...] = jnp.dot(ff[...], ag[0], preferred_element_type=F32).astype(BF)
    store(gv, gv_h)
    k = gather(1, k)
    vz2 = second_z(0, vy1)
    k = forward(1, k)
    loads["kf"].wait()
    ky1, kz1 = factor(1, kf, k)
    vy2 = second_y(0, vz1)
    loads["ef"].wait()
    gk[...] = jnp.dot(ef[...], ag[1], preferred_element_type=F32).astype(BF)
    store(gk, gk_h)
    kz2 = second_z(1, ky1)
    finish(0, vy2, vz2)
    store(gfac.at[0], gvf_h)
    ky2 = second_y(1, kz1)
    finish(1, ky2, kz2)
    store(gfac.at[1], gkf_h)
    for cp in sent:
        cp.wait_send()
    for cp in outs:
        cp.wait()


def per_device(q, kf, vf, kp, vp, ef, ff, do):
    full = jax.ShapeDtypeStruct((TOK, COLS), BF)
    fac = jax.ShapeDtypeStruct((TOK, DH), BF)
    hbm = pl.BlockSpec(memory_space=pl.ANY)
    vm = pltpu.VMEM
    big = vm((TOK, COLS), BF)
    square = vm((TOK, ROWS), BF)
    return pl.pallas_call(
        kernel,
        name="fused_backward",
        out_shape=(full, full, full, fac, fac),
        in_specs=[hbm] * 8,
        out_specs=[hbm] * 5,
        scratch_shapes=[
            big, big, big, big, big, square, square, big,
            vm((4, ROWS, TOK), F32),
            vm((2, ROWS, COLS), F32),
            vm((2, HALF, COLS), BF),
            vm((2, HALF, COLS), BF),
            vm((2, HALF, COLS), BF),
            vm((2, 7, BLK, COLS), BF),
            vm((2, ROWS, COLS), BF),
            vm((2, 8, R1, DH), BF),
            vm((2, 8, R2, DH), BF),
            vm((2, 3, 2, R1, DH), BF),
            vm((2, 4, R2, DH), BF),
            vm((2, R1, DH), F32),
            vm((2, R1, DH), BF),
            vm((2, R1, DH), BF),
            vm((2, 4, R2, DH), BF),
            vm((2, 3, R2, DH), BF),
            big, big, big,
            vm((2, TOK, DH), BF),
            pltpu.SemaphoreType.DMA((8,)),
            pltpu.SemaphoreType.DMA((5,)),
            pltpu.SemaphoreType.DMA((2, NSEM)),
            pltpu.SemaphoreType.DMA((2, NSEM)),
        ],
        compiler_params=pltpu.CompilerParams(
            collective_id=0, has_side_effects=True, vmem_limit_bytes=60 << 20
        ),
    )(q, kf, vf, kp, vp, ef, ff, do)


def solution(mesh):
    whole = P("ctx", "head")
    placed = (
        whole, whole, whole, P(None, "head"), P(None, "head"),
        P("ctx", None), P("ctx", None), whole,
    )
    return jax.shard_map(
        per_device, mesh=mesh, in_specs=placed, out_specs=(whole,) * 5, check_vma=False
    )
```

time: 338 us -> 95.2 us (0.28)
  waiting for transfers between devices: 164 us -> 0 us
  Pallas kernels: 0 us -> 88.6 us
  blocking collectives: 83.5 us -> 0 us
  matrix products: 48.3 us -> 0 us
  between operations: 14.1 us -> 0.66 us
  local copies, waits for them, and re-layouts: 18.4 us -> 5.77 us
  other arithmetic: 9.07 us -> 0 us
    reduce_scatter x2 -> x0, waiting for transfers between devices: 164 us -> none  [the longest x1 91.8 us: per_device(): lax.psum_scatter(kfactor_part, 'head', scatter_dimension=1, tiled=True)]
    pallas_call x0 -> x1, Pallas kernels: none -> 88.6 us  [per_device(): pl.pallas_call(kernel, name='fused_backward', out_shape=(full, full, full...]
    psum x1 -> x0, blocking collectives: 83.5 us -> none  [per_device(): dkp_sum, dvp_sum = lax.psum((dkp_part, dvp_part), 'ctx')]
    dot_general x9 -> x0, matrix products: 38.2 us -> none  [the longest x1 7.45 us: per_device(): jnp.einsum('nhd,rhd->hnr', grad_blocks, value_blocks, preferred_element_t...]
    sub x1 -> x0, matrix products: 10.1 us -> none  [per_device(): probs = jax.nn.softmax(scores, axis=-1)]
    convert_element_type x3 -> x0, other arithmetic: 9.07 us -> none  [the longest x1 6.93 us: per_device(): probs_low = probs.astype(jnp.bfloat16)]
    reshape x3 -> x0, local copies, waits for them, and re-layouts: 6.93 us -> none  [the longest x1 2.41 us: per_device(): query_blocks = queries.reshape(tok_rows, heads_here, DH)]
    unnamed x18 -> x13, local copies, waits for them, and re-layouts: 11.4 us -> 5.77 us
  transfers between devices with their start and end apart: 2 -> 0, of which waited for: 2 -> 0; matrix products, arithmetic and copies ran while one was open for 7% -> 0% of each run, Pallas kernels for 0% -> 0%
where the time goes in v1:
time: 95.2 us; the launch traced here: 95 us
  Pallas kernels  88.6 us (93%)
  local copies, waits for them, and re-layouts  5.77 us (6%)
    pallas_call x1, Pallas kernels, per_device(): pl.pallas_call(kernel, name='fused_backward', out_shape=(full, full, full...  88.6 us
    unnamed x13, local copies, waits for them, and re-layouts  5.77 us

profile of v1, /device:TPU:1, one launch (start us, length us, event | category | flops | bytes accessed | tf_op | source)
XLA Modules:
  0.0 95.0 jit_solution(7187506239238724321)
XLA Ops:
  0.6 88.6 %fused_backward.1 = (bf16[1024,512]{1,0:T(8,128)(2,1)}, bf16[1024,512]{1,0:T(8,128)(2,1)}, bf16[1024,512]{1,0:T(8,128)(2,1)}, bf16[1024,128]{1,0:T(8,128)(2,1)}, bf16[1024,128]{1,0:T(8,128)(2,1)}) custom-call(bf16[1024,512]{1,0:T(8,128)(2,1)} %q_h.1, bf16[1024,512]{1,0:T(8,128)(2,1)} %kf_h.1, bf16[1024,512]{1,0:T(8,128)(2,1)} %vf_h.1, ...), custom_call_target="tpu_custom_call" | custom-call | tf_op jit(solution)/shard_map/fused_backward/pallas_call | solution.py:245
  89.3 0.0 copy-start.1
  89.3 0.0 copy-start
  89.3 2.4 %copy.18 = bf16[1024,512]{1,0:T(8,128)(2,1)} copy(bf16[1024,512]{1,0:T(8,128)(2,1)} %get-tuple-element.10) | data formatting | bytes 2097152
  91.7 0.0 copy-done.1
  91.7 0.0 copy-start.3
  91.7 0.0 copy-start.2
  91.7 1.0 %copy.19 = bf16[1024,512]{1,0:T(8,128)(2,1)} copy(bf16[1024,512]{1,0:T(8,128)(2,1)S(1)} %copy-done.1) | data formatting | bytes 2097152
  92.7 0.0 copy-done
  92.7 1.0 %copy.20 = bf16[1024,512]{1,0:T(8,128)(2,1)} copy(bf16[1024,512]{1,0:T(8,128)(2,1)S(1)} %copy-done) | data formatting | bytes 2097152
  93.6 0.0 copy-done.3
  93.6 0.7 copy.21
  94.3 0.0 copy-done.2
  94.3 0.7 copy.22
Async XLA Ops:
  89.3 2.4 %copy-start.1 = (bf16[1024,512]{1,0:T(8,128)(2,1)S(1)}, bf16[1024,512]{1,0:T(8,128)(2,1)}, u32[]{:S(2)}) copy-start(bf16[1024,512]{1,0:T(8,128)(2,1)} %get-tuple-element.11) | copy-start | bytes 3145732
  89.3 3.4 %copy-start = (bf16[1024,512]{1,0:T(8,128)(2,1)S(1)}, bf16[1024,512]{1,0:T(8,128)(2,1)}, u32[]{:S(2)}) copy-start(bf16[1024,512]{1,0:T(8,128)(2,1)} %get-tuple-element.12) | copy-start | bytes 3145732
  91.7 1.9 %copy-start.3 = (bf16[1024,128]{1,0:T(8,128)(2,1)S(1)}, bf16[1024,128]{1,0:T(8,128)(2,1)}, u32[]{:S(2)}) copy-start(bf16[1024,128]{1,0:T(8,128)(2,1)} %get-tuple-element.13) | copy-start | bytes 786436
  91.7 2.7 %copy-start.2 = (bf16[1024,128]{1,0:T(8,128)(2,1)S(1)}, bf16[1024,128]{1,0:T(8,128)(2,1)}, u32[]{:S(2)}) copy-start(bf16[1024,128]{1,0:T(8,128)(2,1)} %get-tuple-element.14) | copy-start | bytes 786436

commit v2 on v1

v2 whole, which is shorter than its diff:
```python
import functools

import jax
import jax.numpy as jnp
from jax import lax
from jax.experimental import pallas as pl
from jax.experimental.pallas import tpu as pltpu
from jax.sharding import PartitionSpec as P

DH = 128
SCALE = DH ** (-0.5)
SCALE_LOG2 = SCALE * 1.4426950408889634
BF = jnp.bfloat16
F32 = jnp.float32
MESH = pl.DeviceIdType.MESH
NT = (((1,), (1,)), ((), ()))

TOK = 1024
ROWS = 1024
COLS = 512
HALF = ROWS // 2
BLK = HALF // 4
QUART = ROWS // 4

CORE, RS, YX, AG, FWD, SEL, SEL2, Z1, Y1, FULL, NSEM = 0, 1, 4, 5, 8, 9, 10, 32, 35, 37, 45


def kernel(
    q_h, kf_h, vf_h, kp_h, vp_h, e_h, f_h, do_h,
    gq, gk, gv, gkf, gvf,
    q, kf, vf, kp, vp, ef, ff, do,
    probs, acc, xs, xr, rs, rr, part, yb, yx, ag, vf2, kf2, osel, ssel, pag, pb, zv, zk, own1, ys, yr,
    in_sem, ssem, rsem,
):
    ctx = lax.axis_index("ctx")
    head = lax.axis_index("head")
    yh, x, core = ctx // 8, (ctx // 2) % 4, ctx % 2
    z, yl = head // 2, head % 2

    def x_dev(d):
        px = (x + d) % 4
        return px, (yh * 8 + px * 2 + core, head)

    def z_dev(d):
        pz = (z + d) % 4
        return pz, (ctx, pz * 2 + yl)

    par, zi = z % 2, z // 2
    other_par = (ctx, (zi * 2 + (1 - par)) * 2 + yl)
    other_zi = (ctx, ((1 - zi) * 2 + par) * 2 + yl)
    other_yh = ((1 - yh) * 8 + x * 2 + core, head)
    other_core = (yh * 8 + x * 2 + (1 - core), head)
    other_yl = (ctx, z * 2 + (1 - yl))

    bar = pltpu.get_barrier_semaphore()
    peers = [other_core, other_yl, other_yh]
    peers += [x_dev(d)[1] for d in (1, 2, 3)] + [z_dev(d)[1] for d in (1, 2, 3)]
    for p in peers:
        pl.semaphore_signal(bar, inc=1, device_id=p, device_id_type=MESH)

    loads = {}
    for i, (name, src, dst) in enumerate((
        ("q", q_h, q), ("kp", kp_h, kp), ("do", do_h, do), ("vp", vp_h, vp),
        ("vf", vf_h, vf), ("ff", f_h, ff), ("kf", kf_h, kf), ("ef", e_h, ef),
    )):
        loads[name] = pltpu.make_async_copy(src, dst, in_sem.at[i])
        if i < 3:
            loads[name].start()

    def wide(c):
        return slice(c * 2 * DH, (c + 1) * 2 * DH)

    def cols(h):
        return slice(h * DH, (h + 1) * DH)

    def stage_a(h):
        s = lax.dot_general(kp[:, cols(h)], q[:, cols(h)], NT, preferred_element_type=F32)
        m = jnp.max(s, axis=0, keepdims=True)
        e = jnp.exp2((s - m) * SCALE_LOG2)
        l = jnp.sum(e, axis=0, keepdims=True)
        p = e * (1.0 / l)
        probs[h] = p
        acc[0, :, cols(h)] = jnp.dot(p.astype(BF), do[:, cols(h)], preferred_element_type=F32)

    def stage_b(h):
        dp = lax.dot_general(vp[:, cols(h)], do[:, cols(h)], NT, preferred_element_type=F32)
        p = probs[h]
        delta = jnp.sum(p.astype(BF).astype(F32) * dp, axis=0, keepdims=True)
        ds = (p * (dp - delta) * SCALE).astype(BF)
        acc[1, :, cols(h)] = jnp.dot(ds, q[:, cols(h)], preferred_element_type=F32)
        g = jnp.dot(kp[:, cols(h)].T, ds, preferred_element_type=F32)
        gq[:, cols(h)] = g.T.astype(BF)

    sent = []
    pending = []

    def arrive(cp):
        pending[:] = [c for c in pending if c is not cp]
        cp.wait_recv()

    def remote(src, dst, w, slot, dev):
        cp = pltpu.make_async_remote_copy(
            src, dst, ssem.at[w, slot], rsem.at[w, slot], device_id=dev, device_id_type=MESH
        )
        cp.start()
        sent.append(cp)
        pending.append(cp)
        return cp

    mine = pl.multiple_of(core * HALF, HALF)
    theirs = pl.multiple_of((1 - core) * HALF, HALF)
    own_row = pl.multiple_of(core * HALF + x * BLK, BLK)
    own_blk = pl.multiple_of(x * BLK, BLK)

    def swap_cores(w, c):
        xs[w, c] = acc[w, pl.ds(theirs, HALF), wide(c)].astype(BF)
        return [remote(xs.at[w, c], xr.at[w, c], w, 16 * c + CORE, other_core)]

    def scatter(w, c, before):
        arrive(before[0])
        rs[w, c] = (acc[w, pl.ds(mine, HALF), wide(c)] + xr[w, c].astype(F32)).astype(BF)
        out = []
        for d in (1, 2, 3):
            px, dev = x_dev(d)
            src = rs.at[w, c, pl.ds(pl.multiple_of(px * BLK, BLK), BLK), :]
            out.append(remote(src, rr.at[w, c, d - 1], w, 16 * c + RS + d - 1, dev))
        return out

    def exchange(w, c, before):
        total = acc[w, pl.ds(own_row, BLK), wide(c)] + xr[w, c, pl.ds(own_blk, BLK), :].astype(F32)
        for cp in before:
            arrive(cp)
        for d in range(3):
            total = total + rr[w, c, d].astype(F32)
        part[w, c] = total
        yb[w, c] = total.astype(BF)
        return [remote(yb.at[w, c], yx.at[w, c], w, 16 * c + YX, other_yh)]

    def gather(w, c, before):
        arrive(before[0])
        ag[w, c, pl.ds(own_row, BLK), :] = (part[w, c] + yx[w, c].astype(F32)).astype(BF)
        block = ag.at[w, c, pl.ds(own_row, BLK), :]
        return [remote(block, block, w, 16 * c + AG + d - 1, x_dev(d)[1]) for d in (1, 2, 3)]

    def picked(w, c, h, flip):
        if w == 0:
            p = (1 - par) if flip else par
            return ag[0, c, pl.ds(pl.multiple_of((2 * h + p) * QUART, QUART), QUART), :]
        p = (1 - yl) if flip else yl
        return jnp.concatenate([
            ag[1, c, pl.ds(pl.multiple_of((2 * h + i) * QUART + p * DH, DH), DH), :] for i in (0, 1)
        ], axis=0)

    pick = pl.ds(pl.multiple_of(core * QUART, QUART), QUART)

    def forward(w, c, before):
        for cp in before:
            arrive(cp)
        block = ag.at[w, c, pl.ds(mine, HALF), :]
        out = [remote(block, block, w, 16 * c + FWD, other_core)]
        ssel[w, c] = picked(w, c, core, True)
        dev = other_par if w == 0 else other_yl
        out.append(remote(ssel.at[w, c], pag.at[w, c, pick, :], w, 16 * c + SEL, dev))
        return out

    def forward_picked(w, c, before):
        arrive(before[1])
        block = pag.at[w, c, pick, :]
        return [before[0], remote(block, block, w, 16 * c + SEL2, other_core)]

    def own_product(w, full, c0, c1):
        arrive(c0[0])
        arrive(c1[0])
        for c in range(2):
            for h in range(2):
                osel[w, c, h * QUART : (h + 1) * QUART, :] = picked(w, c, h, False)
        probs[w, :, :HALF] = sum(
            lax.dot_general(full[:, wide(c)], osel[w, c], NT, preferred_element_type=F32)
            for c in range(2)
        )

    def product(w, full2, c0, c1):
        arrive(c0[1])
        arrive(c1[1])
        for cp in early[w]:
            arrive(cp)
        for t in range(2):
            rows = slice(t * HALF, (t + 1) * HALF)
            prod = probs[w, rows, :HALF]
            for c in range(2):
                prod = prod + lax.dot_general(
                    full2[rows, wide(c)], pag[w, c], NT, preferred_element_type=F32
                )
            for n in range(4):
                pb[w, n, rows, :] = prod[:, n * DH : (n + 1) * DH].astype(BF)
            if w == 0:
                src = pb.at[0, pl.ds((1 - zi) * 2, 2), rows, :]
                yield remote(src, zv.at[:, rows, :], 0, Z1 + t, other_zi)

    def factor_v(c0, c1):
        return list(product(0, vf2, c0, c1))

    def factor_k(c0, c1):
        for _ in product(1, kf2, c0, c1):
            pass
        out = []
        for d in (1, 2, 3):
            pz, dev = z_dev(d)
            out.append(remote(pb.at[1, pz], zk.at[d - 1], 1, Z1 + d - 1, dev))
        return out

    def second_v(t, cp):
        arrive(cp)
        rows = slice(t * HALF, (t + 1) * HALF)

        def total(b):
            return pb[0, zi * 2 + b, rows, :].astype(F32) + zv[b, rows, :].astype(F32)

        ys[rows, :] = total(1 - yl).astype(BF)
        out = remote(ys.at[rows, :], yr.at[rows, :], 0, Y1 + t, other_yl)
        own1[rows, :] = total(yl)
        return out

    def finish_v(cps):
        for cp in cps:
            arrive(cp)
        gvf[...] = (own1[...] + yr[...].astype(F32)).astype(BF)

    def finish_k(cps):
        t = pb[1, z].astype(F32)
        for d in range(3):
            arrive(cps[d])
            t = t + zk[d].astype(F32)
        gkf[...] = t.astype(BF)

    early = ([], [])

    def early_v():
        early[0].append(remote(vf_h, vf2, 0, FULL, other_par))

    def early_k(i):
        rows = slice(i * DH, (i + 1) * DH)
        early[1].append(remote(kf_h.at[rows, :], kf2.at[rows, :], 1, FULL + i, other_yl))

    def back(w, fac, out):
        for c in range(2):
            out[:, wide(c)] = jnp.dot(fac[...], ag[w, c], preferred_element_type=F32).astype(BF)

    pl.semaphore_wait(bar, len(peers))
    early_v()
    for i in range(3):
        early_k(i)
    for name in ("q", "kp", "do"):
        loads[name].wait()
    for name in ("vp", "vf", "ff", "kf", "ef"):
        loads[name].start()
    stage_a(0)
    stage_a(1)
    v0 = swap_cores(0, 0)
    stage_a(2)
    v0 = scatter(0, 0, v0)
    stage_a(3)
    v1 = swap_cores(0, 1)
    loads["vp"].wait()
    stage_b(0)
    v1 = scatter(0, 1, v1)
    stage_b(1)
    v0 = exchange(0, 0, v0)
    k0 = swap_cores(1, 0)
    stage_b(2)
    v1 = exchange(0, 1, v1)
    for i in range(3, 6):
        early_k(i)
    v0 = gather(0, 0, v0)
    stage_b(3)
    v1 = gather(0, 1, v1)
    k1 = swap_cores(1, 1)
    k0 = scatter(1, 0, k0)
    v0 = forward(0, 0, v0)
    k1 = scatter(1, 1, k1)
    v1 = forward(0, 1, v1)
    k0 = exchange(1, 0, k0)
    v0 = forward_picked(0, 0, v0)
    loads["vf"].wait()
    own_product(0, vf, v0, v1)
    v1 = forward_picked(0, 1, v1)
    k1 = exchange(1, 1, k1)
    for i in range(6, 8):
        early_k(i)
    k0 = gather(1, 0, k0)
    v = factor_v(v0, v1)
    k1 = gather(1, 1, k1)
    loads["ff"].wait()
    back(0, ff, gv)
    k0 = forward(1, 0, k0)
    k1 = forward(1, 1, k1)
    w0 = second_v(0, v[0])
    k0 = forward_picked(1, 0, k0)
    loads["kf"].wait()
    own_product(1, kf, k0, k1)
    k1 = forward_picked(1, 1, k1)
    w1 = second_v(1, v[1])
    k = factor_k(k0, k1)
    loads["ef"].wait()
    back(1, ef, gk)
    finish_v([w0, w1])
    finish_k(k)
    for cp in sent:
        cp.wait_send()


def hand_on(*refs):
    srcs, dsts, sem = refs[:5], refs[5:10], refs[10]
    copies = [pltpu.make_async_copy(s, d, sem.at[i]) for i, (s, d) in enumerate(zip(srcs, dsts))]
    for cp in copies:
        cp.start()
    for cp in copies:
        cp.wait()


def per_device(q, kf, vf, kp, vp, ef, ff, do):
    full = jax.ShapeDtypeStruct((TOK, COLS), BF)
    fac = jax.ShapeDtypeStruct((TOK, DH), BF)
    hbm = pl.BlockSpec(memory_space=pl.ANY)
    vm = pltpu.VMEM
    big = vm((TOK, COLS), BF)
    square = vm((TOK, ROWS), BF)
    made = pl.pallas_call(
        kernel,
        name="fused_backward",
        out_shape=(
            vm((TOK, COLS), BF), vm((TOK, COLS), BF), vm((TOK, COLS), BF),
            vm((TOK, DH), BF), vm((TOK, DH), BF),
        ),
        in_specs=[hbm] * 8,
        out_specs=[pl.BlockSpec(memory_space=vm)] * 5,
        scratch_shapes=[
            big, big, big, big, big, square, square, big,
            vm((4, ROWS, TOK), F32),
            vm((2, ROWS, COLS), F32),
            vm((2, 2, HALF, 2 * DH), BF),
            vm((2, 2, HALF, 2 * DH), BF),
            vm((2, 2, HALF, 2 * DH), BF),
            vm((2, 2, 3, BLK, 2 * DH), BF),
            vm((2, 2, BLK, 2 * DH), F32),
            vm((2, 2, BLK, 2 * DH), BF),
            vm((2, 2, BLK, 2 * DH), BF),
            vm((2, 2, ROWS, 2 * DH), BF),
            big, big,
            vm((2, 2, HALF, 2 * DH), BF),
            vm((2, 2, QUART, 2 * DH), BF),
            vm((2, 2, HALF, 2 * DH), BF),
            vm((2, 4, TOK, DH), BF),
            vm((2, TOK, DH), BF),
            vm((3, TOK, DH), BF),
            vm((TOK, DH), F32),
            vm((TOK, DH), BF),
            vm((TOK, DH), BF),
            pltpu.SemaphoreType.DMA((8,)),
            pltpu.SemaphoreType.DMA((2, NSEM)),
            pltpu.SemaphoreType.DMA((2, NSEM)),
        ],
        compiler_params=pltpu.CompilerParams(
            collective_id=0, has_side_effects=True, vmem_limit_bytes=54 << 20
        ),
    )(q, kf, vf, kp, vp, ef, ff, do)
    return pl.pallas_call(
        hand_on,
        name="hand_on",
        out_shape=(full, full, full, fac, fac),
        in_specs=[pl.BlockSpec(memory_space=vm)] * 5,
        out_specs=[hbm] * 5,
        scratch_shapes=[pltpu.SemaphoreType.DMA((5,))],
        compiler_params=pltpu.CompilerParams(vmem_limit_bytes=1 << 20),
    )(*made)


def solution(mesh):
    whole = P("ctx", "head")
    placed = (
        whole, whole, whole, P(None, "head"), P(None, "head"),
        P("ctx", None), P("ctx", None), whole,
    )
    return jax.shard_map(
        per_device, mesh=mesh, in_specs=placed, out_specs=(whole,) * 5, check_vma=False
    )
```

time: 95.2 us -> 74 us (0.78)
  Pallas kernels: 88.6 us -> 73.1 us
  local copies, waits for them, and re-layouts: 5.77 us -> 0 us
    pallas_call x1 -> x2, Pallas kernels: 88.6 us -> 73.1 us  [the longest x1 71.2 us: per_device(): pl.pallas_call(kernel, name='fused_backward', out_shape=(vm((TOK, COLS),...]
    unnamed x13 -> x0, local copies, waits for them, and re-layouts: 5.77 us -> none
where the time goes in v2:
time: 74 us; the launch traced here: 73.9 us
  Pallas kernels  73.1 us (99%)
  between operations  0.8 us (1%)
    pallas_call x1, Pallas kernels, per_device(): pl.pallas_call(kernel, name='fused_backward', out_shape=(vm((TOK, COLS),...  71.2 us
    pallas_call x1, Pallas kernels, per_device(): pl.pallas_call(hand_on, name='hand_on', out_shape=(full, full, full, fac,...  1.87 us

profile of v2, /device:TPU:1, one launch (start us, length us, event | category | flops | bytes accessed | tf_op | source)
XLA Modules:
  0.0 73.9 jit_solution(9912642510687230454)
XLA Ops:
  0.6 71.2 %fused_backward.1 = (bf16[1024,512]{1,0:T(8,128)(2,1)S(1)}, bf16[1024,512]{1,0:T(8,128)(2,1)S(1)}, bf16[1024,512]{1,0:T(8,128)(2,1)S(1)}, bf16[1024,128]{1,0:T(8,128)(2,1)S(1)}, bf16[1024,128]{1,0:T(8,128)(2,1)S(1)}) custom-call(bf16[1024,512]{1,0:T(8,128)(2,1)} %q_h.1, bf16[1024,512]{1,0:T(8,128)(2,1)} %kf_h.1, bf16[1024,512]{1,0:T(8,128)(2,1)} %vf_h.1, ...), custom_call_target="tpu_custom_call" | custom-call | tf_op jit(solution)/shard_map/fused_backward/pallas_call | solution.py:328
  71.8 1.9 %hand_on.1 = (bf16[1024,512]{1,0:T(8,128)(2,1)}, bf16[1024,512]{1,0:T(8,128)(2,1)}, bf16[1024,512]{1,0:T(8,128)(2,1)}, bf16[1024,128]{1,0:T(8,128)(2,1)}, bf16[1024,128]{1,0:T(8,128)(2,1)}) custom-call(bf16[1024,512]{1,0:T(8,128)(2,1)S(1)} %get-tuple-element.10.refs_0_, bf16[1024,512]{1,0:T(8,128)(2,1)S(1)} %get-tuple-element.11.refs_1_, ...), custom_call_target="tpu_custom_call" | custom-call | tf_op jit(solution)/shard_map/hand_on/pallas_call | solution.py:367

commit v3 on v2

v3 whole, which is shorter than its diff:
```python
import functools

import jax
import jax.numpy as jnp
from jax import lax
from jax.experimental import pallas as pl
from jax.experimental.pallas import tpu as pltpu
from jax.sharding import PartitionSpec as P

DH = 128
SCALE = DH ** (-0.5)
SCALE_LOG2 = SCALE * 1.4426950408889634
BF = jnp.bfloat16
F32 = jnp.float32
MESH = pl.DeviceIdType.MESH
NT = (((1,), (1,)), ((), ()))

TOK = 1024
ROWS = 1024
COLS = 512
HALF = ROWS // 2
BLK = ROWS // 16
QUART = ROWS // 4

CORE, RS, YX, AG, FWD, SEL, SEL2, Z1, Y1, FULL, NSEM = 0, 1, 4, 5, 8, 9, 10, 32, 36, 37, 45


def kernel(
    q_h, kf_h, vf_h, kp_h, vp_h, e_h, f_h, do_h,
    gq, gk, gv, gkf, gvf,
    q, kf, vf, kp, vp, ef, ff, do,
    probs, acc, xs, xr, hs, rs, rr, part, yb, yx, agp, ag, vf2, kf2, pag, pb, zv, zr, zk, ys, yr,
    in_sem, ssem, rsem,
):
    ctx = lax.axis_index("ctx")
    head = lax.axis_index("head")
    yh, x, core = ctx // 8, (ctx // 2) % 4, ctx % 2
    z, yl = head // 2, head % 2

    def x_dev(d):
        px = (x + d) % 4
        return px, (yh * 8 + px * 2 + core, head)

    def z_dev(d):
        pz = (z + d) % 4
        return pz, (ctx, pz * 2 + yl)

    par, zi = z % 2, z // 2
    other_par = (ctx, (zi * 2 + (1 - par)) * 2 + yl)
    other_zi = (ctx, ((1 - zi) * 2 + par) * 2 + yl)
    other_yh = ((1 - yh) * 8 + x * 2 + core, head)
    other_core = (yh * 8 + x * 2 + (1 - core), head)
    other_yl = (ctx, z * 2 + (1 - yl))

    def cols(h):
        return slice(h * DH, (h + 1) * DH)

    head_loads = [
        [
            pltpu.make_async_copy(src.at[:, cols(h)], dst.at[:, cols(h)], in_sem.at[5 + 3 * h + i])
            for i, (src, dst) in enumerate(((q_h, q), (kp_h, kp), (do_h, do)))
        ]
        for h in range(4)
    ]
    for cps in head_loads:
        for cp in cps:
            cp.start()
    loads = {
        name: pltpu.make_async_copy(src, dst, in_sem.at[i])
        for i, (name, src, dst) in enumerate((
            ("vp", vp_h, vp), ("vf", vf_h, vf), ("ff", f_h, ff), ("kf", kf_h, kf), ("ef", e_h, ef),
        ))
    }

    bar = pltpu.get_barrier_semaphore()
    peers = [other_core, other_yl, other_yh]
    peers += [x_dev(d)[1] for d in (1, 2, 3)] + [z_dev(d)[1] for d in (1, 2, 3)]
    for p in peers:
        pl.semaphore_signal(bar, inc=1, device_id=p, device_id_type=MESH)

    def stage_a(h):
        for cp in head_loads[h]:
            cp.wait()
        s = lax.dot_general(kp[:, cols(h)], q[:, cols(h)], NT, preferred_element_type=F32)
        m = jnp.max(s, axis=0, keepdims=True)
        e = jnp.exp2((s - m) * SCALE_LOG2)
        l = jnp.sum(e, axis=0, keepdims=True)
        p = e * (1.0 / l)
        probs[h] = p
        acc[0, :, cols(h)] = jnp.dot(p.astype(BF), do[:, cols(h)], preferred_element_type=F32)

    def stage_b(h):
        dp = lax.dot_general(vp[:, cols(h)], do[:, cols(h)], NT, preferred_element_type=F32)
        p = probs[h]
        delta = jnp.sum(p.astype(BF).astype(F32) * dp, axis=0, keepdims=True)
        ds = (p * (dp - delta) * SCALE).astype(BF)
        acc[1, :, cols(h)] = jnp.dot(ds, q[:, cols(h)], preferred_element_type=F32)
        g = jnp.dot(kp[:, cols(h)].T, ds, preferred_element_type=F32)
        gq[:, cols(h)] = g.T.astype(BF)

    sent = []
    pending = []

    def arrive(cp):
        pending[:] = [c for c in pending if c is not cp]
        cp.wait_recv()

    def remote(src, dst, w, slot, dev):
        cp = pltpu.make_async_remote_copy(
            src, dst, ssem.at[w, slot], rsem.at[w, slot], device_id=dev, device_id_type=MESH
        )
        cp.start()
        sent.append(cp)
        pending.append(cp)
        return cp

    def natural(w, t, h, i):
        if w == 0:
            j = (2 * h + i) * 2 + ((1 - yl) if t == 0 else yl)
        else:
            j = ((z + 2 - t + 2 * h) % 4) * 2 + i
        return pl.ds(pl.multiple_of(j * DH, DH), DH)

    def half(w, t, h):
        return jnp.concatenate([acc[w, natural(w, t, h, i), :] for i in (0, 1)], axis=0)

    def at(start, size):
        return pl.ds(pl.multiple_of(start, size), size)

    pick = (par, yl)
    pick_dev = (other_par, other_yl)

    def swap_cores(w, t):
        xs[w, t] = half(w, t, 1 - core).astype(BF)
        return [remote(xs.at[w, t], xr.at[w, t], w, 16 * t + CORE, other_core)]

    def scatter(w, t, before):
        arrive(before[0])
        total = half(w, t, core) + xr[w, t].astype(F32)
        hs[w, t] = total
        rs[w, t] = total.astype(BF)
        out = []
        for d in (1, 2, 3):
            px, dev = x_dev(d)
            src = rs.at[w, t, at(px * BLK, BLK), :]
            out.append(remote(src, rr.at[w, t, d - 1], w, 16 * t + RS + d - 1, dev))
        return out

    def exchange(w, t, before):
        total = hs[w, t, at(x * BLK, BLK), :]
        for cp in before:
            arrive(cp)
        for d in range(3):
            total = total + rr[w, t, d].astype(F32)
        part[w, t] = total
        yb[w, t] = total.astype(BF)
        return [remote(yb.at[w, t], yx.at[w, t], w, 16 * t + YX, other_yh)]

    def gather(w, t, before):
        arrive(before[0])
        rows = at(core * QUART + x * BLK, BLK)
        agp[w, t, rows, :] = (part[w, t] + yx[w, t].astype(F32)).astype(BF)
        block = agp.at[w, t, rows, :]
        return [remote(block, block, w, 16 * t + AG + d - 1, x_dev(d)[1]) for d in (1, 2, 3)]

    def forward(w, t, before):
        for cp in before:
            arrive(cp)
        src = agp.at[w, t, at((2 * core + 1 - pick[w]) * DH, DH), :]
        dst = pag.at[w, t, at(core * DH, DH), :]
        sel = remote(src, dst, w, 16 * t + SEL, pick_dev[w])
        block = agp.at[w, t, at(core * QUART, QUART), :]
        return [remote(block, block, w, 16 * t + FWD, other_core), sel]

    def forward_picked(w, t, before):
        arrive(before[1])
        block = pag.at[w, t, at(core * DH, DH), :]
        return [before[0], remote(block, block, w, 16 * t + SEL2, other_core)]

    def own_product(w, t, full, before):
        arrive(before[0])
        rows = jnp.concatenate(
            [agp[w, t, at((2 * h + pick[w]) * DH, DH), :] for h in (0, 1)], axis=0
        )
        probs[2 * w + t, :, :QUART] = lax.dot_general(
            full[...], rows, NT, preferred_element_type=F32
        )
        for h in range(2):
            for i in range(2):
                b = 2 * h + i
                ag[w, natural(w, t, h, i), :] = agp[w, t, b * DH : (b + 1) * DH, :]

    def product(w, t, full2, before, relay=()):
        arrive(before[1])
        for cp in early[w]:
            if t == 0:
                arrive(cp)
        prod = probs[2 * w + t, :, :QUART] + lax.dot_general(
            full2[...], pag[w, t], NT, preferred_element_type=F32
        )
        blocks = [prod[:, h * DH : (h + 1) * DH] for h in range(2)]
        for cp in relay:
            arrive(cp)
        if relay:
            blocks[0] = jnp.concatenate(
                [blocks[0][:HALF] + zr[0].astype(F32), blocks[0][HALF:]], axis=0
            )
            blocks[1] = jnp.concatenate(
                [blocks[1][:HALF], blocks[1][HALF:] + zr[1].astype(F32)], axis=0
            )
        for h in range(2):
            pb[w, t, h] = blocks[h].astype(BF)

    def factor_v(t, before):
        product(0, t, vf2, before)
        return remote(pb.at[0, t, 1 - zi], zv.at[t], 0, Z1 + t, other_zi)

    def factor_k(before):
        product(1, 0, kf2, before)
        return [
            remote(pb.at[1, 0, 0, i * HALF : (i + 1) * HALF, :], zr.at[i], 1, Z1 + i, z_dev(d)[1])
            for i, d in ((0, 1), (1, 3))
        ]

    def relay_k(before, relay):
        product(1, 1, kf2, before, relay)
        return [
            remote(pb.at[1, 1, i], zk.at[i], 1, Z1 + 2 + i, z_dev(d)[1])
            for i, d in ((0, 1), (1, 3))
        ]

    def total_v(t, cp):
        arrive(cp)
        return pb[0, t, zi].astype(F32) + zv[t].astype(F32)

    def second_v(cp):
        ys[...] = total_v(0, cp).astype(BF)
        return remote(ys, yr, 0, Y1, other_yl)

    def finish_v(cp, y1):
        total = total_v(1, cp)
        arrive(y1)
        gvf[...] = (total + yr[...].astype(F32)).astype(BF)

    def finish_k(cps):
        t = pb[1, 0, 1].astype(F32)
        for i in range(2):
            arrive(cps[i])
            t = t + zk[i].astype(F32)
        gkf[...] = t.astype(BF)

    early = ([], [])

    def early_v():
        early[0].append(remote(vf_h, vf2, 0, FULL, other_par))

    def early_k(*pieces):
        for i in pieces:
            rows = slice(i * DH, (i + 1) * DH)
            early[1].append(remote(kf_h.at[rows, :], kf2.at[rows, :], 1, FULL + i, other_yl))

    def back(w, fac, out):
        out[...] = jnp.dot(fac[...], ag[w], preferred_element_type=F32).astype(BF)

    stage_a(0)
    for name in ("vp", "vf", "ff", "kf", "ef"):
        loads[name].start()
    stage_a(1)
    pl.semaphore_wait(bar, len(peers))
    early_v()
    early_k(0, 1, 2, 3)
    stage_a(2)
    stage_a(3)
    v0 = swap_cores(0, 0)
    v1 = swap_cores(0, 1)
    loads["vp"].wait()
    stage_b(0)
    v0 = scatter(0, 0, v0)
    v1 = scatter(0, 1, v1)
    stage_b(1)
    stage_b(2)
    v0 = exchange(0, 0, v0)
    stage_b(3)
    k0 = swap_cores(1, 0)
    k1 = swap_cores(1, 1)
    v1 = exchange(0, 1, v1)
    early_k(4, 5, 6, 7)
    v0 = gather(0, 0, v0)
    k0 = scatter(1, 0, k0)
    v1 = gather(0, 1, v1)
    k1 = scatter(1, 1, k1)
    v0 = forward(0, 0, v0)
    k0 = exchange(1, 0, k0)
    v1 = forward(0, 1, v1)
    v0 = forward_picked(0, 0, v0)
    k1 = exchange(1, 1, k1)
    k0 = gather(1, 0, k0)
    loads["vf"].wait()
    own_product(0, 0, vf, v0)
    zv0 = factor_v(0, v0)
    v1 = forward_picked(0, 1, v1)
    own_product(0, 1, vf, v1)
    zv1 = factor_v(1, v1)
    k1 = gather(1, 1, k1)
    k0 = forward(1, 0, k0)
    k1 = forward(1, 1, k1)
    k0 = forward_picked(1, 0, k0)
    loads["kf"].wait()
    own_product(1, 0, kf, k0)
    kz = factor_k(k0)
    k1 = forward_picked(1, 1, k1)
    own_product(1, 1, kf, k1)
    y1 = second_v(zv0)
    loads["ff"].wait()
    back(0, ff, gv)
    kz = relay_k(k1, kz)
    finish_v(zv1, y1)
    loads["ef"].wait()
    back(1, ef, gk)
    finish_k(kz)
    for cp in sent:
        cp.wait_send()


def hand_on(*refs):
    srcs, dsts, sem = refs[:5], refs[5:10], refs[10]
    copies = [pltpu.make_async_copy(s, d, sem.at[i]) for i, (s, d) in enumerate(zip(srcs, dsts))]
    for cp in copies:
        cp.start()
    for cp in copies:
        cp.wait()


def per_device(q, kf, vf, kp, vp, ef, ff, do):
    full = jax.ShapeDtypeStruct((TOK, COLS), BF)
    fac = jax.ShapeDtypeStruct((TOK, DH), BF)
    hbm = pl.BlockSpec(memory_space=pl.ANY)
    vm = pltpu.VMEM
    big = vm((TOK, COLS), BF)
    square = vm((TOK, ROWS), BF)
    made = pl.pallas_call(
        kernel,
        name="fused_backward",
        out_shape=(
            vm((TOK, COLS), BF), vm((TOK, COLS), BF), vm((TOK, COLS), BF),
            vm((TOK, DH), BF), vm((TOK, DH), BF),
        ),
        in_specs=[hbm] * 8,
        out_specs=[pl.BlockSpec(memory_space=vm)] * 5,
        scratch_shapes=[
            big, big, big, big, big, square, square, big,
            vm((4, ROWS, TOK), F32),
            vm((2, ROWS, COLS), F32),
            vm((2, 2, QUART, COLS), BF),
            vm((2, 2, QUART, COLS), BF),
            vm((2, 2, QUART, COLS), F32),
            vm((2, 2, QUART, COLS), BF),
            vm((2, 2, 3, BLK, COLS), BF),
            vm((2, 2, BLK, COLS), F32),
            vm((2, 2, BLK, COLS), BF),
            vm((2, 2, BLK, COLS), BF),
            vm((2, 2, HALF, COLS), BF),
            vm((2, ROWS, COLS), BF),
            big, big,
            vm((2, 2, QUART, COLS), BF),
            vm((2, 2, 2, TOK, DH), BF),
            vm((2, TOK, DH), BF),
            vm((2, HALF, DH), BF),
            vm((2, TOK, DH), BF),
            vm((TOK, DH), BF),
            vm((TOK, DH), BF),
            pltpu.SemaphoreType.DMA((17,)),
            pltpu.SemaphoreType.DMA((2, NSEM)),
            pltpu.SemaphoreType.DMA((2, NSEM)),
        ],
        compiler_params=pltpu.CompilerParams(
            collective_id=0, has_side_effects=True, vmem_limit_bytes=57 << 20
        ),
    )(q, kf, vf, kp, vp, ef, ff, do)
    return pl.pallas_call(
        hand_on,
        name="hand_on",
        out_shape=(full, full, full, fac, fac),
        in_specs=[pl.BlockSpec(memory_space=vm)] * 5,
        out_specs=[hbm] * 5,
        scratch_shapes=[pltpu.SemaphoreType.DMA((5,))],
        compiler_params=pltpu.CompilerParams(vmem_limit_bytes=1 << 20),
    )(*made)


def solution(mesh):
    whole = P("ctx", "head")
    placed = (
        whole, whole, whole, P(None, "head"), P(None, "head"),
        P("ctx", None), P("ctx", None), whole,
    )
    return jax.shard_map(
        per_device, mesh=mesh, in_specs=placed, out_specs=(whole,) * 5, check_vma=False
    )
```

time: 74 us -> 70.6 us (0.954)
  Pallas kernels: 73.1 us -> 69.7 us
    pallas_call x1, Pallas kernels: 71.2 us -> 67.9 us  [per_device(): pl.pallas_call(kernel, name='fused_backward', out_shape=(vm((TOK, COLS),...]
where the time goes in v3:
time: 70.6 us; the launch traced here: 70.5 us
  Pallas kernels  69.7 us (99%)
  between operations  0.8 us (1%)
    pallas_call x1, Pallas kernels, per_device(): pl.pallas_call(kernel, name='fused_backward', out_shape=(vm((TOK, COLS),...  67.9 us
    pallas_call x1, Pallas kernels, per_device(): pl.pallas_call(hand_on, name='hand_on', out_shape=(full, full, full, fac,...  1.87 us

profile of v3, /device:TPU:1, one launch (start us, length us, event | category | flops | bytes accessed | tf_op | source)
XLA Modules:
  0.0 70.5 jit_solution(3639283703016705777)
XLA Ops:
  0.6 67.9 %fused_backward.1 = (bf16[1024,512]{1,0:T(8,128)(2,1)S(1)}, bf16[1024,512]{1,0:T(8,128)(2,1)S(1)}, bf16[1024,512]{1,0:T(8,128)(2,1)S(1)}, bf16[1024,128]{1,0:T(8,128)(2,1)S(1)}, bf16[1024,128]{1,0:T(8,128)(2,1)S(1)}) custom-call(bf16[1024,512]{1,0:T(8,128)(2,1)} %q_h.1, bf16[1024,512]{1,0:T(8,128)(2,1)} %kf_h.1, bf16[1024,512]{1,0:T(8,128)(2,1)} %vf_h.1, ...), custom_call_target="tpu_custom_call" | custom-call | tf_op jit(solution)/shard_map/fused_backward/pallas_call | solution.py:341
  68.5 1.9 %hand_on.1 = (bf16[1024,512]{1,0:T(8,128)(2,1)}, bf16[1024,512]{1,0:T(8,128)(2,1)}, bf16[1024,512]{1,0:T(8,128)(2,1)}, bf16[1024,128]{1,0:T(8,128)(2,1)}, bf16[1024,128]{1,0:T(8,128)(2,1)}) custom-call(bf16[1024,512]{1,0:T(8,128)(2,1)S(1)} %get-tuple-element.10.refs_0_, bf16[1024,512]{1,0:T(8,128)(2,1)S(1)} %get-tuple-element.11.refs_1_, ...), custom_call_target="tpu_custom_call" | custom-call | tf_op jit(solution)/shard_map/hand_on/pallas_call | solution.py:380

commit v4 on v3

--- a/solution.py
+++ b/solution.py
@@ -22,7 +22,7 @@
 BLK = ROWS // 16
 QUART = ROWS // 4
 
-CORE, RS, YX, AG, FWD, SEL, SEL2, Z1, Y1, FULL, NSEM = 0, 1, 4, 5, 8, 9, 10, 32, 36, 37, 45
+CORE, RS, YX, AG, FWD, SEL, SEL2, Z1, Y1, FULL, NSEM = 0, 1, 4, 5, 8, 9, 10, 32, 38, 39, 47
 
 
 def kernel(
@@ -140,7 +140,7 @@
         hs[w, t] = total
         rs[w, t] = total.astype(BF)
         out = []
-        for d in (1, 2, 3):
+        for d in (2, 1, 3):
             px, dev = x_dev(d)
             src = rs.at[w, t, at(px * BLK, BLK), :]
             out.append(remote(src, rr.at[w, t, d - 1], w, 16 * t + RS + d - 1, dev))
@@ -161,7 +161,7 @@
         rows = at(core * QUART + x * BLK, BLK)
         agp[w, t, rows, :] = (part[w, t] + yx[w, t].astype(F32)).astype(BF)
         block = agp.at[w, t, rows, :]
-        return [remote(block, block, w, 16 * t + AG + d - 1, x_dev(d)[1]) for d in (1, 2, 3)]
+        return [remote(block, block, w, 16 * t + AG + d - 1, x_dev(d)[1]) for d in (2, 1, 3)]
 
     def forward(w, t, before):
         for cp in before:
@@ -185,12 +185,8 @@
         probs[2 * w + t, :, :QUART] = lax.dot_general(
             full[...], rows, NT, preferred_element_type=F32
         )
-        for h in range(2):
-            for i in range(2):
-                b = 2 * h + i
-                ag[w, natural(w, t, h, i), :] = agp[w, t, b * DH : (b + 1) * DH, :]
-
-    def product(w, t, full2, before, relay=()):
+
+    def product(w, t, full2, before):
         arrive(before[1])
         for cp in early[w]:
             if t == 0:
@@ -199,15 +195,8 @@
             full2[...], pag[w, t], NT, preferred_element_type=F32
         )
         blocks = [prod[:, h * DH : (h + 1) * DH] for h in range(2)]
-        for cp in relay:
-            arrive(cp)
-        if relay:
-            blocks[0] = jnp.concatenate(
-                [blocks[0][:HALF] + zr[0].astype(F32), blocks[0][HALF:]], axis=0
-            )
-            blocks[1] = jnp.concatenate(
-                [blocks[1][:HALF], blocks[1][HALF:] + zr[1].astype(F32)], axis=0
-            )
+        if w == 1 and t == 1:
+            return blocks
         for h in range(2):
             pb[w, t, h] = blocks[h].astype(BF)
 
@@ -223,11 +212,24 @@
         ]
 
     def relay_k(before, relay):
-        product(1, 1, kf2, before, relay)
-        return [
-            remote(pb.at[1, 1, i], zk.at[i], 1, Z1 + 2 + i, z_dev(d)[1])
-            for i, d in ((0, 1), (1, 3))
-        ]
+        blocks = product(1, 1, kf2, before)
+        halves = (slice(0, HALF), slice(HALF, TOK))
+        out = []
+
+        def send(i, rows, slot):
+            src, dst = pb.at[1, 1, i, rows, :], zk.at[i, rows, :]
+            out.append(remote(src, dst, 1, Z1 + slot, z_dev(1 + 2 * i)[1]))
+
+        for i in range(2):
+            rows = halves[1 - i]
+            pb[1, 1, i, rows, :] = blocks[i][rows].astype(BF)
+            send(i, rows, 2 + i)
+        for i in range(2):
+            rows = halves[i]
+            arrive(relay[i])
+            pb[1, 1, i, rows, :] = (blocks[i][rows] + zr[i].astype(F32)).astype(BF)
+            send(i, rows, 4 + i)
+        return out
 
     def total_v(t, cp):
         arrive(cp)
@@ -244,8 +246,9 @@
 
     def finish_k(cps):
         t = pb[1, 0, 1].astype(F32)
+        for cp in cps:
+            arrive(cp)
         for i in range(2):
-            arrive(cps[i])
             t = t + zk[i].astype(F32)
         gkf[...] = t.astype(BF)
 
@@ -260,6 +263,10 @@
             early[1].append(remote(kf_h.at[rows, :], kf2.at[rows, :], 1, FULL + i, other_yl))
 
     def back(w, fac, out):
+        for t in range(2):
+            for b in range(4):
+                rows = natural(w, t, b // 2, b % 2)
+                ag[w, rows, :] = agp[w, t, b * DH : (b + 1) * DH, :]
         out[...] = jnp.dot(fac[...], ag[w], preferred_element_type=F32).astype(BF)
 
     stage_a(0)
@@ -293,10 +300,10 @@
     k0 = exchange(1, 0, k0)
     v1 = forward(0, 1, v1)
     v0 = forward_picked(0, 0, v0)
-    k1 = exchange(1, 1, k1)
-    k0 = gather(1, 0, k0)
     loads["vf"].wait()
     own_product(0, 0, vf, v0)
+    k0 = gather(1, 0, k0)
+    k1 = exchange(1, 1, k1)
     zv0 = factor_v(0, v0)
     v1 = forward_picked(0, 1, v1)
     own_product(0, 1, vf, v1)
@@ -308,9 +315,9 @@
     loads["kf"].wait()
     own_product(1, 0, kf, k0)
     kz = factor_k(k0)
+    y1 = second_v(zv0)
     k1 = forward_picked(1, 1, k1)
     own_product(1, 1, kf, k1)
-    y1 = second_v(zv0)
     loads["ff"].wait()
     back(0, ff, gv)
     kz = relay_k(k1, kz)

time: 70.6 us -> 68 us (0.963)
  Pallas kernels: 69.7 us -> 66.5 us
    pallas_call x1, Pallas kernels: 67.9 us -> 64.6 us  [per_device(): pl.pallas_call(kernel, name='fused_backward', out_shape=(vm((TOK, COLS),...]
where the time goes in v4:
time: 68 us; the launch traced here: 67.3 us
  Pallas kernels  66.5 us (98%)
  between operations  0.8 us (1%)
    pallas_call x1, Pallas kernels, per_device(): pl.pallas_call(kernel, name='fused_backward', out_shape=(vm((TOK, COLS),...  64.6 us
    pallas_call x1, Pallas kernels, per_device(): pl.pallas_call(hand_on, name='hand_on', out_shape=(full, full, full, fac,...  1.87 us

profile of v4, /device:TPU:1, one launch (start us, length us, event | category | flops | bytes accessed | tf_op | source)
XLA Modules:
  0.0 67.3 jit_solution(4874441290321230882)
XLA Ops:
  0.6 64.6 %fused_backward.1 = (bf16[1024,512]{1,0:T(8,128)(2,1)S(1)}, bf16[1024,512]{1,0:T(8,128)(2,1)S(1)}, bf16[1024,512]{1,0:T(8,128)(2,1)S(1)}, bf16[1024,128]{1,0:T(8,128)(2,1)S(1)}, bf16[1024,128]{1,0:T(8,128)(2,1)S(1)}) custom-call(bf16[1024,512]{1,0:T(8,128)(2,1)} %q_h.1, bf16[1024,512]{1,0:T(8,128)(2,1)} %kf_h.1, bf16[1024,512]{1,0:T(8,128)(2,1)} %vf_h.1, ...), custom_call_target="tpu_custom_call" | custom-call | tf_op jit(solution)/shard_map/fused_backward/pallas_call | solution.py:348
  65.3 1.9 %hand_on.1 = (bf16[1024,512]{1,0:T(8,128)(2,1)}, bf16[1024,512]{1,0:T(8,128)(2,1)}, bf16[1024,512]{1,0:T(8,128)(2,1)}, bf16[1024,128]{1,0:T(8,128)(2,1)}, bf16[1024,128]{1,0:T(8,128)(2,1)}) custom-call(bf16[1024,512]{1,0:T(8,128)(2,1)S(1)} %get-tuple-element.10.refs_0_, bf16[1024,512]{1,0:T(8,128)(2,1)S(1)} %get-tuple-element.11.refs_1_, ...), custom_call_target="tpu_custom_call" | custom-call | tf_op jit(solution)/shard_map/hand_on/pallas_call | solution.py:387
